TPU v7x, 32 devices: a whole 2x2x4 slice. The times are simulated.
32 devices in a mesh: dp: 8 (over y, x, core), mp: 4 (over z).
Axes of the slice: x: 2, y: 2, z: 4, core: 2. Of those that a mesh axis runs over, the one named last changes fastest.
Arguments:
- acts: bfloat16 [1024, 8192], P('dp', 'mp'), may hold values from -6 to 6
- grads: bfloat16 [1024, 28672], P('dp', 'mp'), may hold values from -6 to 6
- proj_in: bfloat16 [8192, 64], replicated, may hold values from -0.0625 to 0.0625
- block_vals: bfloat16 [128, 128, 64], replicated, may hold values from -0.046875 to 0.046875
- block_index: int32 [128], replicated, may hold values from 0 to 223, as said below
- assign: int32 [8, 128], P('dp'), may hold values from 0 to 127, each once within a row
Outputs:
- features: bfloat16 [1024, 4096], P(('dp', 'mp'))
- factor: float32 [8, 512, 512], P('mp')
Inputs may be any that keep to these rules, and one draw needn't show every extreme that they name: `block_index`: 128 distinct row blocks. Each row of assign names every example of its group once.
All inputs are finite; a program needn't handle non-finite values.
Results may differ from a plain program's by a relative error of at most 0.013.
Values may be sent and summed in bfloat16 or wider, within the bound.
A program may use at most 64 MiB of HBM per device.

v0:
```python
import jax
import jax.numpy as jnp
from jax import lax
from jax.sharding import PartitionSpec as P

FB = 512


DAMPING = 0.05


def upper_factor(matrix):
    return jnp.swapaxes(jnp.linalg.cholesky(matrix), 1, 2)


def shards(acts, grads, proj_in, block_vals, block_index, assign):
    mp_count = lax.axis_size("mp")
    dp_count = lax.axis_size("dp")
    row_order = assign[0]
    ex_rows = acts.shape[0] // mp_count
    block_rows = block_vals.shape[1]
    out_width = block_vals.shape[2]
    own_index = lax.axis_index("mp")
    slice_width = acts.shape[1]
    in_rows = lax.dynamic_slice_in_dim(proj_in, own_index * slice_width, slice_width, 0)
    in_part = jnp.dot(acts, in_rows, preferred_element_type=jnp.float32)
    local_blocks = grads.shape[1] // block_rows
    block_ids = own_index * local_blocks + jnp.arange(local_blocks, dtype=jnp.int32)
    owned_blocks = (block_index[None, :] == block_ids[:, None]).astype(jnp.bfloat16)
    flat_vals = block_vals.reshape(block_vals.shape[0], block_rows * out_width)
    dense_proj = jnp.dot(owned_blocks, flat_vals, preferred_element_type=jnp.float32)
    dense_proj = dense_proj.astype(jnp.bfloat16).reshape(local_blocks * block_rows, out_width)
    out_part = jnp.dot(grads, dense_proj, preferred_element_type=jnp.float32)
    in_full, out_full = (
        lax.psum_scatter(in_part[row_order], "mp", scatter_dimension=0, tiled=True),
        lax.psum_scatter(out_part[row_order], "mp", scatter_dimension=0, tiled=True),
    )
    in_coords = in_full.astype(jnp.bfloat16)
    out_coords = out_full.astype(jnp.bfloat16)
    outer = in_coords.astype(jnp.float32)[:, :, None] * out_coords.astype(jnp.float32)[:, None, :]
    features = outer.reshape(ex_rows, -1).astype(jnp.bfloat16)
    my_columns = lax.all_to_all(features, "mp", split_axis=1, concat_axis=0, tiled=True)
    group_rows = my_columns.shape[0]
    block_count = my_columns.shape[1] // FB
    column_blocks = my_columns.reshape(group_rows, block_count, FB)
    gram_blocks = jnp.einsum(
        "rbi,rbj->bij", column_blocks, column_blocks, preferred_element_type=jnp.float32
    )
    row_total = group_rows * dp_count
    identity = jnp.eye(FB, dtype=jnp.float32)
    summed = lax.psum(gram_blocks.astype(jnp.bfloat16), "dp").astype(jnp.float32)
    factor = upper_factor(summed / row_total + DAMPING * identity)
    return (features, factor)


def solution(mesh):
    return jax.shard_map(
        shards,
        mesh=mesh,
        in_specs=(P("dp", "mp"), P("dp", "mp"), P(), P(), P(), P("dp", None)),
        out_specs=(P(("dp", "mp"), None), P("mp", None, None)),
        check_vma=False,
    )
```

profile of v0, /device:TPU:0, one launch (start us, length us, event | category | flops | bytes accessed | tf_op | source)
XLA Modules:
  0.0 320.7 jit_solution(1495328403758468680)
XLA Ops:
  7.2 4.7 %copy.65 = bf16[128,128,64]{0,2,1:T(8,128)(2,1)} copy(bf16[128,128,64]{1,2,0:T(8,128)(2,1)} %param.9) | data formatting | bytes 4194304 | tf_op args[3]
  11.9 2.5 convolution_convert_fusion
  14.4 3.2 reshape.112
  17.5 2.2 convolution_bitcast_fusion
  19.7 0.1 copy.66
  19.9 1.2 gather_fusion.1
  21.2 1.3 convolution_bitcast_fusion.1
  22.5 0.1 copy.64
  22.6 1.2 gather_fusion
  23.9 19.1 %reduce-scatter.5.cloned.1.call-done = f32[32,64]{1,0:T(8,128)} async-done(((f32[128,64]{1,0:T(8,128)}), f32[32,64]{1,0:T(8,128)}) %reduce-scatter.5.cloned.1.call-update) | async-done | bytes 8208 | tf_op jit(solution)/shard_map/reduce_scatter | solution.py:36
  43.0 0.7 convert_convert_fusion
  43.7 19.4 %reduce-scatter.3.cloned.1.call-done = f32[32,64]{1,0:T(8,128)} async-done(((f32[128,64]{1,0:T(8,128)}), f32[32,64]{1,0:T(8,128)}) %reduce-scatter.3.cloned.1.call-update) | async-done | bytes 8208 | tf_op jit(solution)/shard_map/reduce_scatter | solution.py:35
  63.1 0.7 convert_convert_fusion.1
  63.8 0.3 multiply_convert_fusion
  64.2 0.3 convert_element_type.40
  64.5 0.1 copy.67
  64.6 9.5 %all_to_all.13 = bf16[32,4,1024]{2,0,1:T(8,128)(2,1)S(1)} all-to-all(bf16[32,4,1024]{2,0,1:T(8,128)(2,1)S(1)} %copy.67), channel_id=1, replica_groups=mesh['dp'=8,'mp'=4] {'mp'}, dimensions={1} | all-to-all | bytes 524288 | tf_op jit(solution)/shard_map/all_to_all | solution.py:42
  74.1 0.2 reshape.113
  74.3 1.5 convolution_convert_fusion.1
  75.8 0.8 iota_compare_fusion.1
  76.6 0.1 fusion.1
  76.7 1.2 convert_element_type.39
  77.9 54.1 %all-reduce.3.cloned.1.call-done = bf16[2,512,512]{1,2,0:T(8,128)(2,1)} async-done(((bf16[2,512,512]{1,2,0:T(8,128)(2,1)}), bf16[2,512,512]{1,2,0:T(8,128)(2,1)}) %all-reduce.3.cloned.1.call-update) | async-done | bytes 1048592 | tf_op jit(solution)/shard_map/psum | solution.py:51
  131.9 2.9 multiply_add_fusion
  134.8 2.9 copy.71
  137.7 2.3 fusion
  140.1 1.3 copy-done.1
  141.4 23.5 %custom-call.31 = f32[2,128,128]{2,1,0:T(8,128)S(1)} custom-call(f32[2,128,128]{2,1,0:T(8,128)S(1)} %cholesky.274), custom_call_target="Cholesky" | custom-call | tf_op jit(solution)/shard_map/jit(cholesky)/cholesky | solution.py:13
  164.9 1.6 cholesky.234
  166.5 19.7 %custom-call.32 = f32[2,1,128,128]{2,3,1,0:T(8,128)S(1)} custom-call(f32[2,1,128,128]{3,2,1,0:T(8,128)S(1)} %select_bitcast_fusion.3), custom_call_target="InvertDiagBlocksLowerTriangular" | custom-call | tf_op jit(solution)/shard_map/jit(cholesky)/cholesky | solution.py:13
  186.2 2.2 constant_dynamic-update-slice_fusion.3
  188.4 1.5 convolution_subtract_fusion
  189.9 23.7 %custom-call.33 = f32[2,128,128]{2,1,0:T(8,128)S(1)} custom-call(f32[2,128,128]{2,1,0:T(8,128)S(1)} %cholesky.278), custom_call_target="Cholesky" | custom-call | tf_op jit(solution)/shard_map/jit(cholesky)/cholesky | solution.py:13
  213.6 0.7 select_bitcast_fusion.2
  214.3 19.7 %custom-call.34 = f32[2,1,128,128]{2,3,1,0:T(8,128)S(1)} custom-call(f32[2,1,128,128]{3,2,1,0:T(8,128)S(1)} %get-tuple-element.19), custom_call_target="InvertDiagBlocksLowerTriangular" | custom-call | tf_op jit(solution)/shard_map/jit(cholesky)/cholesky | solution.py:13
  234.0 1.1 convolution_dynamic-update-slice_fusion
  235.1 1.8 convolution_subtract_fusion.1
  236.9 23.5 %custom-call.35 = f32[2,128,128]{2,1,0:T(8,128)S(1)} custom-call(f32[2,128,128]{2,1,0:T(8,128)S(1)} %cholesky.283), custom_call_target="Cholesky" | custom-call | tf_op jit(solution)/shard_map/jit(cholesky)/cholesky | solution.py:13
  260.3 0.7 select_bitcast_fusion.1
  261.0 19.7 %custom-call.36 = f32[2,1,128,128]{2,3,1,0:T(8,128)S(1)} custom-call(f32[2,1,128,128]{3,2,1,0:T(8,128)S(1)} %get-tuple-element.17), custom_call_target="InvertDiagBlocksLowerTriangular" | custom-call | tf_op jit(solution)/shard_map/jit(cholesky)/cholesky | solution.py:13
  280.7 0.9 convolution_dynamic-update-slice_fusion.1
  281.6 1.8 convolution_subtract_fusion.2
  283.4 23.5 %custom-call.37 = f32[2,128,128]{2,1,0:T(8,128)S(1)} custom-call(f32[2,128,128]{2,1,0:T(8,128)S(1)} %convolution_subtract_fusion.2), custom_call_target="Cholesky" | custom-call | tf_op jit(solution)/shard_map/jit(cholesky)/cholesky | solution.py:13
  306.9 0.7 select_reduce_fusion.2
  307.6 0.1 compare_reduce_fusion
  307.7 0.2 compare_reduce_fusion.2
  307.9 3.3 %select_bitcast_fusion = f32[2,512,512]{1,2,0:T(8,128)} fusion(f32[2,512,512]{2,1,0:T(8,128)} %get-tuple-element.16, pred[2]{0:T(512)(128)(4,1)S(1)} %or_or_fusion, pred[512,512]{1,0:T(8,128)(4,1)S(1)} %copy-done.2), kind=kLoop, calls=%fused_computation.5 | loop fusion | flops 1048576 | bytes 4456450 | tf_op jit(solution)/shard_map/transpose | solution.py:13
  311.2 2.9 copy.78
  (27 shorter events, 0.3 us)
Async XLA Ops:
  7.2 10.4 %copy-start = (bf16[128,7168]{1,0:T(8,128)(2,1)S(1)}, bf16[128,7168]{1,0:T(8,128)(2,1)}, u32[]{:S(2)}) copy-start(bf16[128,7168]{1,0:T(8,128)(2,1)} %param.7) | copy-start | bytes 5505028
  7.2 35.8 %reduce-scatter.5.cloned.1.call-start = ((), (), s32[]{:S(2)}) async-start(), calls=%async_computation.4 | async-start | bytes 81920 | tf_op jit(solution)/shard_map/reduce_scatter | solution.py:36
  7.2 4.7 %copy-start.4 = (s32[128]{0:T(128)S(1)}, s32[128]{0:T(128)}, u32[]{:S(2)}) copy-start(s32[128]{0:T(128)} %param.10) | copy-start | bytes 1540
  17.5 2.3 copy-start.5
  17.5 3.7 %copy-start.3 = (bf16[128,2048]{1,0:T(8,128)(2,1)S(1)}, bf16[128,2048]{1,0:T(8,128)(2,1)}, u32[]{:S(2)}) copy-start(bf16[128,2048]{1,0:T(8,128)(2,1)} %param.6) | copy-start | bytes 1572868
  21.1 42.0 %reduce-scatter.3.cloned.1.call-start = ((), (), s32[]{:S(2)}) async-start(), calls=%async_computation.3 | async-start | bytes 81920 | tf_op jit(solution)/shard_map/reduce_scatter | solution.py:35
  23.8 108.1 %all-reduce.3.cloned.1.call-start = ((), (), s32[]{:S(2)}) async-start(), calls=%async_computation.5 | async-start | bytes 2097152 | tf_op jit(solution)/shard_map/psum | solution.py:51
  140.1 1.4 copy-start.1
  234.0 73.9 %copy-start.2 = (pred[512,512]{1,0:T(8,128)(4,1)S(1)}, pred[512,512]{1,0:T(8,128)(4,1)}, u32[]{:S(2)}) copy-start(pred[512,512]{1,0:T(8,128)(4,1)} %iota_compare_fusion.1) | copy-start | bytes 786436
Sparse Core Ops, SparseCore 0:
  21.3 21.6 reduce-scatter.4
  45.9 17.1 reduce-scatter.2
  75.9 56.0 all-reduce.2
where the time goes:
time: 321 us
  other arithmetic  167 us (52%)
  waiting for transfers between devices  92.6 us (29%)
  local copies, waits for them, and re-layouts  21 us (7%)
  matrix products  16.7 us (5%)
  between operations  14 us (4%)
  blocking collectives  9.51 us (3%)
    another operation x16, other arithmetic, upper_factor(): return jnp.swapaxes(jnp.linalg.cholesky(matrix), 1, 2)  155 us
    psum x1, waiting for transfers between devices, shards(): lax.psum(gram_blocks.astype(jnp.bfloat16), 'dp').astype(jnp.float32)  54.1 us
    reduce_scatter x1, waiting for transfers between devices, shards(): lax.psum_scatter(in_part[row_order], 'mp', scatter_dimension=0, tiled=True)  19.4 us
    reduce_scatter x1, waiting for transfers between devices, shards(): lax.psum_scatter(out_part[row_order], 'mp', scatter_dimension=0, tiled=True)  19.1 us
    all_to_all x1, blocking collectives, shards(): lax.all_to_all(features, 'mp', split_axis=1, concat_axis=0, tiled=True)  9.51 us
    another operation x6, matrix products, upper_factor(): return jnp.swapaxes(jnp.linalg.cholesky(matrix), 1, 2)  9.33 us
    unnamed x14, local copies, waits for them, and re-layouts  8.9 us
  transfers between devices with their start and end apart: 3, of which 3 were waited for; matrix products, arithmetic and copies ran while one was open for 2% of the time, Pallas kernels for 0%

commit v1 on v0

v1 whole, which is shorter than its diff:
```python
import functools

import jax
import jax.numpy as jnp
from jax import lax
from jax.experimental import pallas as pl
from jax.experimental.pallas import tpu as pltpu
from jax.sharding import PartitionSpec as P

MESH = pl.DeviceIdType.MESH
FB = 512
DAMPING = 0.05
TILE = 128
STEP = 16
F32 = jnp.float32
BF16 = jnp.bfloat16


def dot_nt(a, b):
    return lax.dot_general(a, b, (((1,), (1,)), ((), ())), preferred_element_type=F32)


def dot_tn(a, b):
    return lax.dot_general(a, b, (((0,), (0,)), ((), ())), preferred_element_type=F32)


def project_kernel(index_ref, assign_ref, acts_ref, grads_ref, proj_ref, vals_ref, out_ref, dense):
    own = lax.axis_index("mp")
    width = acts_ref.shape[1]
    blk = vals_ref.shape[2]
    k_in = proj_ref.shape[0]
    local = grads_ref.shape[1] // blk
    dense[...] = jnp.zeros_like(dense)

    def place(t, carry):
        at = index_ref[t] - own * local
        at = jnp.where((at >= 0) & (at < local), at, local)
        dense[:, pl.ds(pl.multiple_of(at * blk, blk), blk)] = vals_ref[t]
        return carry

    lax.fori_loop(0, vals_ref.shape[0], place, 0, unroll=8)
    cols = pl.ds(pl.multiple_of(own * width, width), width)
    in_part = dot_nt(proj_ref[:, cols], acts_ref[...])
    out_part = dot_nt(dense[:, : local * blk], grads_ref[...])
    rows = acts_ref.shape[0]
    pick = (lax.broadcasted_iota(jnp.int32, (rows, rows), 0) == assign_ref[...]).astype(BF16)
    out_ref[:k_in] = jnp.dot(in_part.astype(BF16), pick, preferred_element_type=F32).astype(BF16)
    out_ref[k_in:] = jnp.dot(out_part.astype(BF16), pick, preferred_element_type=F32).astype(BF16)


def exchange_kernel(mp, dp, k_in, need, part_ref, full_ref, gath_ref, recv, slab, s1, r1, s2, r2):
    m = lax.axis_index("mp")
    d = lax.axis_index("dp")
    barrier = pltpu.get_barrier_semaphore()
    for o in range(1, mp):
        pl.semaphore_signal(barrier, inc=1, device_id=(d, lax.rem(m + o, mp)), device_id_type=MESH)
    for o in range(1, dp):
        pl.semaphore_signal(barrier, inc=1, device_id=(lax.rem(d + o, dp), m), device_id_type=MESH)
    pl.semaphore_wait(barrier, mp + dp - 2)
    copies = []
    for o in range(1, mp):
        copy = pltpu.make_async_remote_copy(
            src_ref=part_ref, dst_ref=recv.at[m], send_sem=s1.at[o - 1], recv_sem=r1.at[o - 1],
            device_id=(d, lax.rem(m + o, mp)), device_id_type=MESH)
        copy.start()
        copies.append(copy)
    recv[m] = part_ref[...]
    for copy in copies:
        copy.wait()
    total = recv[0].astype(F32)
    for j in range(1, mp):
        total = total + recv[j].astype(F32)
    full_ref[...] = total.astype(BF16)
    first = (m * (k_in // mp)) // need * need
    slab[:need] = full_ref[pl.ds(pl.multiple_of(first, need), need), :]
    slab[need:] = full_ref[k_in:, :]
    copies = []
    for o in range(1, dp):
        copy = pltpu.make_async_remote_copy(
            src_ref=slab, dst_ref=gath_ref.at[d], send_sem=s2.at[o - 1], recv_sem=r2.at[o - 1],
            device_id=(lax.rem(d + o, dp), m), device_id_type=MESH)
        copy.start()
        copies.append(copy)
    gath_ref[d] = slab[...]
    for copy in copies:
        copy.wait()


def split(x):
    high = x.astype(BF16).astype(F32)
    return high, x - high


def eliminate(cols, rows):
    sub = lax.broadcasted_iota(jnp.int32, (STEP, TILE), 0)
    scale = jnp.zeros((STEP, TILE), F32)
    for k in range(STEP):
        col = cols[k]
        root = lax.rsqrt(col[k:k + 1, :])
        inv = root * root
        scale = jnp.where(sub == k, root, scale)
        if k == STEP - 1:
            break
        below = jnp.where(sub > k, col, 0.0)
        for j in range(k + 1, STEP):
            cols[j] = cols[j] - (below * col[j:j + 1, :]) * inv
        below = below * inv
        for t in range(len(rows)):
            rows[t] = rows[t] - below * rows[t][k:k + 1, :]
    return [row * scale for row in rows]


def factor_kernel(mp, k_in, k_out, need, gath_ref, full_ref, feat_ref, factor_ref, ft, inf, cov, panel, upper):
    m = lax.axis_index("mp")
    dp, _, ex = gath_ref.shape
    nb = factor_ref.shape[0]
    tiles = FB // TILE
    per = FB // k_out
    skip = m * (k_in // mp) - (m * (k_in // mp)) // need * need

    mine = feat_ref.shape[0]
    pick = (lax.broadcasted_iota(jnp.int32, (mine, ex), 0) + m * mine
            == lax.broadcasted_iota(jnp.int32, (mine, ex), 1)).astype(BF16)
    coords = dot_nt(pick, full_ref[...])
    lane = lax.broadcasted_iota(jnp.int32, (mine, TILE), 1)
    outs = jnp.concatenate([coords[:, k_in:], coords[:, k_in:]], axis=1)
    for t in range(k_in // 2):
        left = jnp.broadcast_to(coords[:, 2 * t:2 * t + 1], (mine, TILE))
        right = jnp.broadcast_to(coords[:, 2 * t + 1:2 * t + 2], (mine, TILE))
        feat_ref[:, t * TILE:(t + 1) * TILE] = (jnp.where(lane < k_out, left, right) * outs).astype(BF16)

    def expand(g, carry):
        inf[...] = gath_ref[g, :need, :].astype(F32)
        out = gath_ref[g, need:, :].astype(F32)
        at = pl.ds(pl.multiple_of(g * ex, ex), ex)
        for p in range(nb * per):
            if nb * per == need:
                row = inf[p:p + 1, :]
            else:
                row = inf[pl.ds(skip + p, 1), :]
            ft[p * k_out:(p + 1) * k_out, at] = (row * out).astype(BF16)
        return carry

    lax.fori_loop(0, dp, expand, 0)

    total = dp * ex
    chunk = min(total, 1024)
    half = FB // 2
    diag = jnp.where(lax.broadcasted_iota(jnp.int32, (half, half), 0)
                     == lax.broadcasted_iota(jnp.int32, (half, half), 1), DAMPING, 0.0)
    for c in range(nb):
        for i in range(2):
            for j in range(i, 2):
                def piece(n):
                    at = pl.ds(pl.multiple_of(n * chunk, chunk), chunk)
                    return dot_nt(ft[c * FB + i * half:c * FB + (i + 1) * half, at],
                                  ft[c * FB + j * half:c * FB + (j + 1) * half, at])
                gram = piece(0)
                if total > chunk:
                    gram = lax.fori_loop(1, total // chunk, lambda n, acc: acc + piece(n), gram)
                gram = gram * (1.0 / total)
                if i == j:
                    gram = gram + diag
                cov[c, i * half:(i + 1) * half, j * half:(j + 1) * half] = gram

    def block_row(b, carry):
        at = pl.ds(pl.multiple_of(b * TILE, TILE), TILE)

        def tile_at(t):
            return pl.ds(pl.multiple_of(lax.rem(b + t, tiles) * TILE, TILE), TILE)

        for c in range(nb):
            for t in range(tiles):
                panel[c, t] = cov[c, at, tile_at(t)]
        for s in range(TILE // STEP):
            lo, hi = s * STEP, (s + 1) * STEP
            cols = []
            for c in range(nb):
                pivot = panel[c, 0, lo:hi, :]
                cols.append([jnp.broadcast_to(pivot[:, lo + j:lo + j + 1], (STEP, TILE)) for j in range(STEP)])
            for c in range(nb):
                rows = eliminate(cols[c], [panel[c, t, lo:hi, :] for t in range(tiles)])
                parts = [split(row) for row in rows]
                for t in range(tiles):
                    upper[c, t, lo:hi, :] = rows[t]
                if hi < TILE:
                    h, l = parts[0]
                    left = jnp.concatenate([h, h, l, l], axis=0)[:, hi:].astype(BF16)
                    right = jnp.concatenate(
                        [jnp.concatenate([h, l, h, l], axis=0) for h, l in parts], axis=1).astype(BF16)
                    update = dot_tn(left, right)
                    for t in range(tiles):
                        panel[c, t, hi:, :] = panel[c, t, hi:, :] - update[:, t * TILE:(t + 1) * TILE]
        tri = (lax.broadcasted_iota(jnp.int32, (TILE, TILE), 1)
               >= lax.broadcasted_iota(jnp.int32, (TILE, TILE), 0))
        for c in range(nb):
            factor_ref[c, at, tile_at(0)] = jnp.where(tri, upper[c, 0], 0.0)
            for t in range(1, tiles):
                factor_ref[c, at, tile_at(t)] = jnp.where(b + t < tiles, upper[c, t], 0.0)
        for i in range(1, tiles):
            @pl.when(b + i < tiles)
            def _():
                here = pl.ds(pl.multiple_of(lax.rem(b + i, tiles) * TILE, TILE), TILE)
                for c in range(nb):
                    h, l = split(upper[c, i])
                    left = jnp.concatenate([h, h, l, l], axis=0).astype(BF16)
                    for t in range(i, tiles):
                        h, l = split(upper[c, t])
                        right = jnp.concatenate([h, l, h, l], axis=0).astype(BF16)
                        cov[c, here, tile_at(t)] = cov[c, here, tile_at(t)] - dot_tn(left, right)
        return carry

    lax.fori_loop(0, tiles, block_row, 0)


def shards(acts, grads, proj_in, block_vals, block_index, assign):
    mp = lax.axis_size("mp")
    dp = lax.axis_size("dp")
    ex = acts.shape[0]
    k_in = proj_in.shape[1]
    nblk, blk, k_out = block_vals.shape
    feat = k_in * k_out
    nb = feat // FB // mp
    need = max(16, k_in // mp)
    vmem = pl.BlockSpec(memory_space=pltpu.VMEM)
    part = pl.pallas_call(
        project_kernel,
        out_shape=jax.ShapeDtypeStruct((k_in + k_out, ex), BF16),
        in_specs=[pl.BlockSpec(memory_space=pltpu.SMEM)] + [vmem] * 5,
        out_specs=vmem,
        scratch_shapes=[pltpu.VMEM((k_out, grads.shape[1] + blk), BF16)],
        compiler_params=pltpu.CompilerParams(vmem_limit_bytes=48 << 20),
    )(block_index, assign, acts, grads, proj_in.T, jnp.swapaxes(block_vals, 1, 2))
    full, gath = pl.pallas_call(
        functools.partial(exchange_kernel, mp, dp, k_in, need),
        out_shape=(jax.ShapeDtypeStruct((k_in + k_out, ex), BF16),
                   jax.ShapeDtypeStruct((dp, need + k_out, ex), BF16)),
        in_specs=[vmem],
        out_specs=(vmem, vmem),
        scratch_shapes=[
            pltpu.VMEM((mp, k_in + k_out, ex), BF16),
            pltpu.VMEM((need + k_out, ex), BF16),
            pltpu.SemaphoreType.DMA((mp - 1,)),
            pltpu.SemaphoreType.DMA((mp - 1,)),
            pltpu.SemaphoreType.DMA((dp - 1,)),
            pltpu.SemaphoreType.DMA((dp - 1,)),
        ],
        compiler_params=pltpu.CompilerParams(collective_id=0, has_side_effects=True),
    )(part)
    features, factor = pl.pallas_call(
        functools.partial(factor_kernel, mp, k_in, k_out, need),
        out_shape=(jax.ShapeDtypeStruct((ex // mp, feat), BF16),
                   jax.ShapeDtypeStruct((nb, FB, FB), F32)),
        in_specs=[vmem, vmem],
        out_specs=(vmem, vmem),
        scratch_shapes=[
            pltpu.VMEM((nb * FB, dp * ex), BF16),
            pltpu.VMEM((need, ex), F32),
            pltpu.VMEM((nb, FB, FB), F32),
            pltpu.VMEM((nb, FB // TILE, TILE, TILE), F32),
            pltpu.VMEM((nb, FB // TILE, TILE, TILE), F32),
        ],
        compiler_params=pltpu.CompilerParams(vmem_limit_bytes=48 << 20),
    )(gath, full)
    return features, factor


def solution(mesh):
    return jax.shard_map(
        shards,
        mesh=mesh,
        in_specs=(P("dp", "mp"), P("dp", "mp"), P(), P(), P(), P("dp", None)),
        out_specs=(P(("dp", "mp"), None), P("mp", None, None)),
        check_vma=False,
    )
```

time: 321 us -> 52.2 us (0.16)
  other arithmetic: 167 us -> 0 us
  waiting for transfers between devices: 92.6 us -> 0 us
  Pallas kernels: 0 us -> 42.1 us
  matrix products: 16.7 us -> 0 us
  between operations: 14 us -> 0.66 us
  local copies, waits for them, and re-layouts: 21 us -> 8.95 us
  blocking collectives: 9.51 us -> 0 us
    another operation x16 -> x0, other arithmetic: 155 us -> none  [upper_factor(): return jnp.swapaxes(jnp.linalg.cholesky(matrix), 1, 2)]
    psum x1 -> x0, waiting for transfers between devices: 54.1 us -> none  [shards(): lax.psum(gram_blocks.astype(jnp.bfloat16), 'dp').astype(jnp.float32)]
    pallas_call x0 -> x3, Pallas kernels: none -> 42.1 us  [the longest x1 25.6 us: shards(): pl.pallas_call(functools.partial(factor_kernel, mp, k_in, k_out, need), o...]
    reduce_scatter x2 -> x0, waiting for transfers between devices: 38.5 us -> none  [the longest x1 19.4 us: shards(): lax.psum_scatter(in_part[row_order], 'mp', scatter_dimension=0, tiled=True)]
    all_to_all x1 -> x0, blocking collectives: 9.51 us -> none  [shards(): lax.all_to_all(features, 'mp', split_axis=1, concat_axis=0, tiled=True)]
    another operation x6 -> x0, matrix products: 9.33 us -> none  [upper_factor(): return jnp.swapaxes(jnp.linalg.cholesky(matrix), 1, 2)]
    dot_general x4 -> x0, matrix products: 7.37 us -> none  [the longest x1 2.47 us: shards(): jnp.dot(owned_blocks, flat_vals, preferred_element_type=jnp.float32)]
    transpose x1 -> x0, other arithmetic: 3.35 us -> none  [upper_factor(): return jnp.swapaxes(jnp.linalg.cholesky(matrix), 1, 2)]
  transfers between devices with their start and end apart: 3 -> 0, of which waited for: 3 -> 0; matrix products, arithmetic and copies ran while one was open for 2% -> 0% of each run, Pallas kernels for 0% -> 0%
where the time goes in v1:
time: 52.2 us; the launch traced here: 51.7 us
  Pallas kernels  42.1 us (81%)
  local copies, waits for them, and re-layouts  8.95 us (17%)
  between operations  0.66 us (1%)
    pallas_call x1, Pallas kernels, shards(): pl.pallas_call(functools.partial(factor_kernel, mp, k_in, k_out, need), o...  25.6 us
    pallas_call x1, Pallas kernels, shards(): pl.pallas_call(functools.partial(exchange_kernel, mp, dp, k_in, need), ou...  14.3 us
    unnamed x18, local copies, waits for them, and re-layouts  8.95 us
    pallas_call x1, Pallas kernels, shards(): pl.pallas_call(project_kernel, out_shape=jax.ShapeDtypeStruct((k_in + k_o...  2.23 us

profile of v1, /device:TPU:0, one launch (start us, length us, event | category | flops | bytes accessed | tf_op | source)
XLA Modules:
  0.0 51.7 jit_solution(10448975025283271060)
XLA Ops:
  0.6 0.0 copy-start
  0.6 1.6 %copy-done = bf16[128,128,64]{1,2,0:T(8,128)(2,1)S(1)} copy-done((bf16[128,128,64]{1,2,0:T(8,128)(2,1)S(1)}, bf16[128,128,64]{1,2,0:T(8,128)(2,1)}, u32[]{:S(2)}) %copy-start) | copy-done | bytes 2097176
  2.2 0.0 copy-start.1
  2.2 1.5 %copy-done.1 = bf16[128,7168]{1,0:T(8,128)(2,1)S(1)} copy-done((bf16[128,7168]{1,0:T(8,128)(2,1)S(1)}, bf16[128,7168]{1,0:T(8,128)(2,1)}, u32[]{:S(2)}) %copy-start.1) | copy-done | bytes 1835032
  3.7 0.0 copy-start.2
  3.7 1.2 %copy-done.2 = bf16[8192,64]{0,1:T(8,128)(2,1)S(1)} copy-done((bf16[8192,64]{0,1:T(8,128)(2,1)S(1)}, bf16[8192,64]{0,1:T(8,128)(2,1)}, u32[]{:S(2)}) %copy-start.2) | copy-done | bytes 1048600
  4.9 0.0 copy-start.3
  5.0 1.0 %copy-done.3 = bf16[128,2048]{1,0:T(8,128)(2,1)S(1)} copy-done((bf16[128,2048]{1,0:T(8,128)(2,1)S(1)}, bf16[128,2048]{1,0:T(8,128)(2,1)}, u32[]{:S(2)}) %copy-start.3) | copy-done | bytes 524312
  6.0 0.0 copy-start.7
  6.0 0.7 %copy-done.7 = s32[128]{0:T(128)S(1)} copy-done((s32[128]{0:T(128)S(1)}, s32[128]{0:T(128)}, u32[]{:S(2)}) %copy-start.7) | copy-done | bytes 536
  6.6 0.0 copy-start.8
  6.6 0.7 %copy-done.8 = s32[1,128]{1,0:T(1,128)S(1)} copy-done((s32[1,128]{1,0:T(1,128)S(1)}, s32[1,128]{1,0:T(1,128)}, u32[]{:S(2)}) %copy-start.8) | copy-done | bytes 536
  7.3 2.2 %shard_map.77.part_ref = bf16[128,128]{1,0:T(8,128)(2,1)S(1)} custom-call(s32[128]{0:T(128)S(1)} %copy-done.7, s32[1,128]{1,0:T(1,128)S(1)} %copy-done.8, bf16[128,2048]{1,0:T(8,128)(2,1)S(1)} %copy-done.3, bf16[128,7168]{1,0:T(8,128)(2,1)S(1)} %copy-done.1, bf16[64,8192]{1,0:T(8,128)(2,1)S(1)} %bitcast.3, bf16[128,64,128]{2,1,0:T(8,128)(2,1)S(1)} %bitcast.2), custom_call_target="tpu_custom_call" | custom-call | tf_op jit(solution)/shard_map/pallas_call | solution.py:226
  9.5 0.0 copy-start.5
  9.5 0.6 %copy-done.5 = bf16[128,128]{1,0:T(8,128)(2,1)} copy-done((bf16[128,128]{1,0:T(8,128)(2,1)}, bf16[128,128]{1,0:T(8,128)(2,1)S(1)}, u32[]{:S(2)}) %copy-start.5) | copy-done | bytes 32792
  10.2 14.3 %shard_map.78 = (bf16[128,128]{1,0:T(8,128)(2,1)}, bf16[8,80,128]{2,1,0:T(8,128)(2,1)}) custom-call(bf16[128,128]{1,0:T(8,128)(2,1)} %copy-done.5), custom_call_target="tpu_custom_call" | custom-call | tf_op jit(solution)/shard_map/pallas_call | solution.py:234
  24.5 0.0 copy-start.4
  24.5 0.9 %copy-done.4 = bf16[8,80,128]{2,1,0:T(8,128)(2,1)S(1)} copy-done((bf16[8,80,128]{2,1,0:T(8,128)(2,1)S(1)}, bf16[8,80,128]{2,1,0:T(8,128)(2,1)}, u32[]{:S(2)}) %copy-start.4) | copy-done | bytes 163864
  25.4 0.0 copy-start.6
  25.4 0.8 %copy-done.6 = bf16[128,128]{1,0:T(8,128)(2,1)S(1)} copy-done((bf16[128,128]{1,0:T(8,128)(2,1)S(1)}, bf16[128,128]{1,0:T(8,128)(2,1)}, u32[]{:S(2)}) %copy-start.6) | copy-done | bytes 32792
  26.2 25.6 %shard_map.79 = (bf16[32,4096]{1,0:T(8,128)(2,1)}, f32[2,512,512]{2,1,0:T(8,128)}) custom-call(bf16[8,80,128]{2,1,0:T(8,128)(2,1)S(1)} %copy-done.4, bf16[128,128]{1,0:T(8,128)(2,1)S(1)} %copy-done.6), custom_call_target="tpu_custom_call" | custom-call | tf_op jit(solution)/shard_map/pallas_call | solution.py:250
Async XLA Ops:
  0.6 1.6 %copy-start = (bf16[128,128,64]{1,2,0:T(8,128)(2,1)S(1)}, bf16[128,128,64]{1,2,0:T(8,128)(2,1)}, u32[]{:S(2)}) copy-start(bf16[128,128,64]{1,2,0:T(8,128)(2,1)} %param.9) | copy-start | bytes 6291460
  2.2 1.5 %copy-start.1 = (bf16[128,7168]{1,0:T(8,128)(2,1)S(1)}, bf16[128,7168]{1,0:T(8,128)(2,1)}, u32[]{:S(2)}) copy-start(bf16[128,7168]{1,0:T(8,128)(2,1)} %grads_ref.1) | copy-start | bytes 5505028
  3.7 1.2 %copy-start.2 = (bf16[8192,64]{0,1:T(8,128)(2,1)S(1)}, bf16[8192,64]{0,1:T(8,128)(2,1)}, u32[]{:S(2)}) copy-start(bf16[8192,64]{0,1:T(8,128)(2,1)} %param.8) | copy-start | bytes 3145732
  4.9 1.0 %copy-start.3 = (bf16[128,2048]{1,0:T(8,128)(2,1)S(1)}, bf16[128,2048]{1,0:T(8,128)(2,1)}, u32[]{:S(2)}) copy-start(bf16[128,2048]{1,0:T(8,128)(2,1)} %acts_ref.1) | copy-start | bytes 1572868
  6.0 0.7 %copy-start.7 = (s32[128]{0:T(128)S(1)}, s32[128]{0:T(128)}, u32[]{:S(2)}) copy-start(s32[128]{0:T(128)} %index_ref.1) | copy-start | bytes 1540
  6.6 0.7 %copy-start.8 = (s32[1,128]{1,0:T(1,128)S(1)}, s32[1,128]{1,0:T(1,128)}, u32[]{:S(2)}) copy-start(s32[1,128]{1,0:T(1,128)} %assign_ref.1) | copy-start | bytes 1540
  9.5 0.6 %copy-start.5 = (bf16[128,128]{1,0:T(8,128)(2,1)}, bf16[128,128]{1,0:T(8,128)(2,1)S(1)}, u32[]{:S(2)}) copy-start(bf16[128,128]{1,0:T(8,128)(2,1)S(1)} %shard_map.77.part_ref) | copy-start | bytes 98308
  24.5 0.9 %copy-start.4 = (bf16[8,80,128]{2,1,0:T(8,128)(2,1)S(1)}, bf16[8,80,128]{2,1,0:T(8,128)(2,1)}, u32[]{:S(2)}) copy-start(bf16[8,80,128]{2,1,0:T(8,128)(2,1)} %get-tuple-element.4.gath_ref) | copy-start | bytes 491524
  25.4 0.8 %copy-start.6 = (bf16[128,128]{1,0:T(8,128)(2,1)S(1)}, bf16[128,128]{1,0:T(8,128)(2,1)}, u32[]{:S(2)}) copy-start(bf16[128,128]{1,0:T(8,128)(2,1)} %get-tuple-element.5.full_ref) | copy-start | bytes 98308

commit v2 on v1

--- a/solution.py
+++ b/solution.py
@@ -24,31 +24,8 @@
     return lax.dot_general(a, b, (((0,), (0,)), ((), ())), preferred_element_type=F32)
 
 
-def project_kernel(index_ref, assign_ref, acts_ref, grads_ref, proj_ref, vals_ref, out_ref, dense):
-    own = lax.axis_index("mp")
-    width = acts_ref.shape[1]
-    blk = vals_ref.shape[2]
-    k_in = proj_ref.shape[0]
-    local = grads_ref.shape[1] // blk
-    dense[...] = jnp.zeros_like(dense)
-
-    def place(t, carry):
-        at = index_ref[t] - own * local
-        at = jnp.where((at >= 0) & (at < local), at, local)
-        dense[:, pl.ds(pl.multiple_of(at * blk, blk), blk)] = vals_ref[t]
-        return carry
-
-    lax.fori_loop(0, vals_ref.shape[0], place, 0, unroll=8)
-    cols = pl.ds(pl.multiple_of(own * width, width), width)
-    in_part = dot_nt(proj_ref[:, cols], acts_ref[...])
-    out_part = dot_nt(dense[:, : local * blk], grads_ref[...])
-    rows = acts_ref.shape[0]
-    pick = (lax.broadcasted_iota(jnp.int32, (rows, rows), 0) == assign_ref[...]).astype(BF16)
-    out_ref[:k_in] = jnp.dot(in_part.astype(BF16), pick, preferred_element_type=F32).astype(BF16)
-    out_ref[k_in:] = jnp.dot(out_part.astype(BF16), pick, preferred_element_type=F32).astype(BF16)
-
-
-def exchange_kernel(mp, dp, k_in, need, part_ref, full_ref, gath_ref, recv, slab, s1, r1, s2, r2):
+def coords_kernel(mp, dp, need, inverse_ref, assign_ref, acts_hbm, grads_hbm, proj_hbm, vals_hbm, full_ref, gath_ref,
+                  acts, grads, proj, vals, dense, part, recv, slab, ins, s1, r1, s2, r2):
     m = lax.axis_index("mp")
     d = lax.axis_index("dp")
     barrier = pltpu.get_barrier_semaphore()
@@ -56,24 +33,62 @@
         pl.semaphore_signal(barrier, inc=1, device_id=(d, lax.rem(m + o, mp)), device_id_type=MESH)
     for o in range(1, dp):
         pl.semaphore_signal(barrier, inc=1, device_id=(lax.rem(d + o, dp), m), device_id_type=MESH)
+    ex, width = acts.shape
+    k_in = proj.shape[0]
+    nblk, k_out, blk = vals_hbm.shape
+    local = grads.shape[1] // blk
+    cols = pl.ds(pl.multiple_of(m * width, width), width)
+    loads = [
+        pltpu.make_async_copy(proj_hbm.at[:, cols], proj, ins.at[0]),
+        pltpu.make_async_copy(acts_hbm, acts, ins.at[1]),
+        pltpu.make_async_copy(vals_hbm, vals.at[pl.ds(0, nblk)], ins.at[2]),
+        pltpu.make_async_copy(grads_hbm, grads, ins.at[3]),
+    ]
+    for load in loads:
+        load.start()
+    vals[nblk] = jnp.zeros((k_out, blk), BF16)
+    pick = (lax.broadcasted_iota(jnp.int32, (ex, ex), 0) == assign_ref[...]).astype(BF16)
+
+    def send(lo, hi, at):
+        copies = []
+        for o in range(1, mp):
+            copy = pltpu.make_async_remote_copy(
+                src_ref=part.at[pl.ds(lo, hi - lo)], dst_ref=recv.at[m, pl.ds(lo, hi - lo)],
+                send_sem=s1.at[at, o - 1], recv_sem=r1.at[at, o - 1],
+                device_id=(d, lax.rem(m + o, mp)), device_id_type=MESH)
+            copy.start()
+            copies.append(copy)
+        recv[m, lo:hi] = part[lo:hi]
+        return copies
+
+    loads[0].wait()
+    loads[1].wait()
+    in_part = dot_nt(proj[...], acts[...])
+    part[:k_in] = jnp.dot(in_part.astype(BF16), pick, preferred_element_type=F32).astype(BF16)
     pl.semaphore_wait(barrier, mp + dp - 2)
-    copies = []
-    for o in range(1, mp):
-        copy = pltpu.make_async_remote_copy(
-            src_ref=part_ref, dst_ref=recv.at[m], send_sem=s1.at[o - 1], recv_sem=r1.at[o - 1],
-            device_id=(d, lax.rem(m + o, mp)), device_id_type=MESH)
-        copy.start()
-        copies.append(copy)
-    recv[m] = part_ref[...]
-    for copy in copies:
+    in_copies = send(0, k_in, 0)
+    loads[2].wait()
+    for b in range(local):
+        dense[:, b * blk:(b + 1) * blk] = vals[inverse_ref[b]]
+    loads[3].wait()
+    out_part = dot_nt(dense[...], grads[...])
+    part[k_in:] = jnp.dot(out_part.astype(BF16), pick, preferred_element_type=F32).astype(BF16)
+    out_copies = send(k_in, k_in + k_out, 1)
+
+    def add_up(lo, hi):
+        total = recv[0, lo:hi].astype(F32)
+        for j in range(1, mp):
+            total = total + recv[j, lo:hi].astype(F32)
+        return total.astype(BF16)
+
+    for copy in in_copies:
         copy.wait()
-    total = recv[0].astype(F32)
-    for j in range(1, mp):
-        total = total + recv[j].astype(F32)
-    full_ref[...] = total.astype(BF16)
+    full_ref[:k_in] = add_up(0, k_in)
     first = (m * (k_in // mp)) // need * need
     slab[:need] = full_ref[pl.ds(pl.multiple_of(first, need), need), :]
-    slab[need:] = full_ref[k_in:, :]
+    for copy in out_copies:
+        copy.wait()
+    slab[need:] = add_up(k_in, k_in + k_out)
     copies = []
     for o in range(1, dp):
         copy = pltpu.make_async_remote_copy(
@@ -81,6 +96,7 @@
             device_id=(lax.rem(d + o, dp), m), device_id_type=MESH)
         copy.start()
         copies.append(copy)
+    full_ref[k_in:] = slab[need:]
     gath_ref[d] = slab[...]
     for copy in copies:
         copy.wait()
@@ -91,32 +107,58 @@
     return high, x - high
 
 
-def eliminate(cols, rows):
-    sub = lax.broadcasted_iota(jnp.int32, (STEP, TILE), 0)
-    scale = jnp.zeros((STEP, TILE), F32)
+def eliminate(heads, tails, rows):
+    half = STEP // 2
+    sub = lax.broadcasted_iota(jnp.int32, (half, TILE), 0)
+    scale = [jnp.zeros((half, TILE), F32) for _ in range(2)]
+    tops = [row[:half] for row in rows]
+    ends = [row[half:] for row in rows]
     for k in range(STEP):
-        col = cols[k]
-        root = lax.rsqrt(col[k:k + 1, :])
+        low, at = k < half, k % half
+        pivot = heads[k] if low else tails[k]
+        root = jnp.broadcast_to(lax.rsqrt(pivot[at:at + 1, :]), (half, TILE))
         inv = root * root
-        scale = jnp.where(sub == k, root, scale)
+        scale[k // half] = jnp.where(sub == at, root, scale[k // half])
         if k == STEP - 1:
             break
-        below = jnp.where(sub > k, col, 0.0)
-        for j in range(k + 1, STEP):
-            cols[j] = cols[j] - (below * col[j:j + 1, :]) * inv
-        below = below * inv
-        for t in range(len(rows)):
-            rows[t] = rows[t] - below * rows[t][k:k + 1, :]
-    return [row * scale for row in rows]
-
-
-def factor_kernel(mp, k_in, k_out, need, gath_ref, full_ref, feat_ref, factor_ref, ft, inf, cov, panel, upper):
+        end = tails[k] * inv
+        if low:
+            top = heads[k] * inv
+            for j in range(k + 1, half):
+                entry = heads[k][j:j + 1, :]
+                heads[j] = heads[j] - top * entry
+                tails[j] = tails[j] - end * entry
+            for j in range(half, STEP):
+                tails[j] = tails[j] - end * tails[k][j - half:j - half + 1, :]
+            top = jnp.where(sub > at, top, 0.0)
+            for t in range(len(rows)):
+                row = tops[t][at:at + 1, :]
+                if at < half - 1:
+                    tops[t] = tops[t] - top * row
+                ends[t] = ends[t] - end * row
+        else:
+            for j in range(k + 1, STEP):
+                tails[j] = tails[j] - end * tails[k][j - half:j - half + 1, :]
+            end = jnp.where(sub > at, end, 0.0)
+            for t in range(len(rows)):
+                ends[t] = ends[t] - end * ends[t][at:at + 1, :]
+    return [jnp.concatenate([top * scale[0], end * scale[1]], axis=0) for top, end in zip(tops, ends)]
+
+
+def factor_kernel(mp, k_in, k_out, need, gath_hbm, full_hbm, feat_hbm, factor_hbm,
+                  gath_ref, full_ref, feat_ref, factor_ref, ft, inf, cov, panel, upper, ins, fsem, osem):
     m = lax.axis_index("mp")
     dp, _, ex = gath_ref.shape
     nb = factor_ref.shape[0]
     tiles = FB // TILE
     per = FB // k_out
     skip = m * (k_in // mp) - (m * (k_in // mp)) // need * need
+
+    full_load = pltpu.make_async_copy(full_hbm, full_ref, ins.at[0])
+    gath_load = pltpu.make_async_copy(gath_hbm, gath_ref, ins.at[1])
+    full_load.start()
+    gath_load.start()
+    full_load.wait()
 
     mine = feat_ref.shape[0]
     pick = (lax.broadcasted_iota(jnp.int32, (mine, ex), 0) + m * mine
@@ -128,6 +170,10 @@
         left = jnp.broadcast_to(coords[:, 2 * t:2 * t + 1], (mine, TILE))
         right = jnp.broadcast_to(coords[:, 2 * t + 1:2 * t + 2], (mine, TILE))
         feat_ref[:, t * TILE:(t + 1) * TILE] = (jnp.where(lane < k_out, left, right) * outs).astype(BF16)
+
+    feat_store = pltpu.make_async_copy(feat_ref, feat_hbm, fsem)
+    feat_store.start()
+    gath_load.wait()
 
     def expand(g, carry):
         inf[...] = gath_ref[g, :need, :].astype(F32)
@@ -177,9 +223,12 @@
             cols = []
             for c in range(nb):
                 pivot = panel[c, 0, lo:hi, :]
-                cols.append([jnp.broadcast_to(pivot[:, lo + j:lo + j + 1], (STEP, TILE)) for j in range(STEP)])
+                half = STEP // 2
+                cols.append((
+                    [jnp.broadcast_to(pivot[:half, lo + j:lo + j + 1], (half, TILE)) for j in range(half)],
+                    [jnp.broadcast_to(pivot[half:, lo + j:lo + j + 1], (half, TILE)) for j in range(STEP)]))
             for c in range(nb):
-                rows = eliminate(cols[c], [panel[c, t, lo:hi, :] for t in range(tiles)])
+                rows = eliminate(*cols[c], [panel[c, t, lo:hi, :] for t in range(tiles)])
                 parts = [split(row) for row in rows]
                 for t in range(tiles):
                     upper[c, t, lo:hi, :] = rows[t]
@@ -197,6 +246,7 @@
             factor_ref[c, at, tile_at(0)] = jnp.where(tri, upper[c, 0], 0.0)
             for t in range(1, tiles):
                 factor_ref[c, at, tile_at(t)] = jnp.where(b + t < tiles, upper[c, t], 0.0)
+            pltpu.make_async_copy(factor_ref.at[c, at], factor_hbm.at[c, at], osem.at[c, b]).start()
         for i in range(1, tiles):
             @pl.when(b + i < tiles)
             def _():
@@ -211,6 +261,11 @@
         return carry
 
     lax.fori_loop(0, tiles, block_row, 0)
+    feat_store.wait()
+    for c in range(nb):
+        for b in range(tiles):
+            at = pl.ds(b * TILE, TILE)
+            pltpu.make_async_copy(factor_ref.at[c, at], factor_hbm.at[c, at], osem.at[c, b]).wait()
 
 
 def shards(acts, grads, proj_in, block_vals, block_index, assign):
@@ -223,42 +278,54 @@
     nb = feat // FB // mp
     need = max(16, k_in // mp)
     vmem = pl.BlockSpec(memory_space=pltpu.VMEM)
-    part = pl.pallas_call(
-        project_kernel,
-        out_shape=jax.ShapeDtypeStruct((k_in + k_out, ex), BF16),
-        in_specs=[pl.BlockSpec(memory_space=pltpu.SMEM)] + [vmem] * 5,
-        out_specs=vmem,
-        scratch_shapes=[pltpu.VMEM((k_out, grads.shape[1] + blk), BF16)],
-        compiler_params=pltpu.CompilerParams(vmem_limit_bytes=48 << 20),
-    )(block_index, assign, acts, grads, proj_in.T, jnp.swapaxes(block_vals, 1, 2))
+    hbm = pl.BlockSpec(memory_space=pltpu.HBM)
+    local = grads.shape[1] // blk
+    ids = lax.axis_index("mp") * local + jnp.arange(local, dtype=jnp.int32)
+    order = jnp.arange(nblk, dtype=jnp.int32)
+    inverse = jnp.min(jnp.where(block_index[None, :] == ids[:, None], order[None, :], nblk), axis=1)
     full, gath = pl.pallas_call(
-        functools.partial(exchange_kernel, mp, dp, k_in, need),
+        functools.partial(coords_kernel, mp, dp, need),
         out_shape=(jax.ShapeDtypeStruct((k_in + k_out, ex), BF16),
                    jax.ShapeDtypeStruct((dp, need + k_out, ex), BF16)),
-        in_specs=[vmem],
+        in_specs=[pl.BlockSpec(memory_space=pltpu.SMEM), vmem] + [hbm] * 4,
         out_specs=(vmem, vmem),
         scratch_shapes=[
+            pltpu.VMEM(acts.shape, BF16),
+            pltpu.VMEM(grads.shape, BF16),
+            pltpu.VMEM((k_in, acts.shape[1]), BF16),
+            pltpu.VMEM((nblk + 1, k_out, blk), BF16),
+            pltpu.VMEM((k_out, grads.shape[1]), BF16),
+            pltpu.VMEM((k_in + k_out, ex), BF16),
             pltpu.VMEM((mp, k_in + k_out, ex), BF16),
             pltpu.VMEM((need + k_out, ex), BF16),
-            pltpu.SemaphoreType.DMA((mp - 1,)),
-            pltpu.SemaphoreType.DMA((mp - 1,)),
+            pltpu.SemaphoreType.DMA((4,)),
+            pltpu.SemaphoreType.DMA((2, mp - 1)),
+            pltpu.SemaphoreType.DMA((2, mp - 1)),
             pltpu.SemaphoreType.DMA((dp - 1,)),
             pltpu.SemaphoreType.DMA((dp - 1,)),
         ],
-        compiler_params=pltpu.CompilerParams(collective_id=0, has_side_effects=True),
-    )(part)
+        compiler_params=pltpu.CompilerParams(
+            collective_id=0, has_side_effects=True, vmem_limit_bytes=63 << 20),
+    )(inverse, assign, acts, grads, proj_in.T, jnp.swapaxes(block_vals, 1, 2))
     features, factor = pl.pallas_call(
         functools.partial(factor_kernel, mp, k_in, k_out, need),
         out_shape=(jax.ShapeDtypeStruct((ex // mp, feat), BF16),
                    jax.ShapeDtypeStruct((nb, FB, FB), F32)),
-        in_specs=[vmem, vmem],
-        out_specs=(vmem, vmem),
+        in_specs=[hbm, hbm],
+        out_specs=(hbm, hbm),
         scratch_shapes=[
+            pltpu.VMEM(gath.shape, BF16),
+            pltpu.VMEM(full.shape, BF16),
+            pltpu.VMEM((ex // mp, feat), BF16),
+            pltpu.VMEM((nb, FB, FB), F32),
             pltpu.VMEM((nb * FB, dp * ex), BF16),
             pltpu.VMEM((need, ex), F32),
             pltpu.VMEM((nb, FB, FB), F32),
             pltpu.VMEM((nb, FB // TILE, TILE, TILE), F32),
             pltpu.VMEM((nb, FB // TILE, TILE, TILE), F32),
+            pltpu.SemaphoreType.DMA((2,)),
+            pltpu.SemaphoreType.DMA(()),
+            pltpu.SemaphoreType.DMA((nb, FB // TILE)),
         ],
         compiler_params=pltpu.CompilerParams(vmem_limit_bytes=48 << 20),
     )(gath, full)

time: 52.2 us -> 43.4 us (0.83)
  local copies, waits for them, and re-layouts: 8.95 us -> 1.67 us
  Pallas kernels: 42.1 us -> 39.5 us
  other arithmetic: 0 us -> 1.36 us
    unnamed x18 -> x4, local copies, waits for them, and re-layouts: 8.95 us -> 1.67 us
    pallas_call x1, Pallas kernels: 25.6 us -> 23.4 us  [shards(): pl.pallas_call(functools.partial(factor_kernel, mp, k_in, k_out, need), o...]
    reduce_min x0 -> x1, other arithmetic: none -> 1.36 us  [shards(): jnp.min(jnp.where(block_index[None, :] == ids[:, None], order[None, :], n...]
    pallas_call x2 -> x1, Pallas kernels: 16.5 us -> 16.1 us  [shards(): pl.pallas_call(functools.partial(coords_kernel, mp, dp, need), out_shape=...]
where the time goes in v2:
time: 43.4 us; the launch traced here: 43.1 us
  Pallas kernels  39.5 us (91%)
  local copies, waits for them, and re-layouts  1.67 us (4%)
  other arithmetic  1.36 us (3%)
  between operations  0.66 us (2%)
    pallas_call x1, Pallas kernels, shards(): pl.pallas_call(functools.partial(factor_kernel, mp, k_in, k_out, need), o...  23.4 us
    pallas_call x1, Pallas kernels, shards(): pl.pallas_call(functools.partial(coords_kernel, mp, dp, need), out_shape=...  16.1 us
    unnamed x4, local copies, waits for them, and re-layouts  1.67 us
    reduce_min x1, other arithmetic, shards(): jnp.min(jnp.where(block_index[None, :] == ids[:, None], order[None, :], n...  1.36 us

profile of v2, /device:TPU:0, one launch (start us, length us, event | category | flops | bytes accessed | tf_op | source)
XLA Modules:
  0.0 43.1 jit_solution(5909499967876041336)
XLA Ops:
  0.6 1.4 %select_reduce_fusion.inverse_ref = s32[56]{0:T(128)} fusion(s32[128]{0:T(128)} %param.10, s32[56]{0:T(128)S(1)} %iota_add_fusion), kind=kLoop, calls=%fused_computation | loop fusion | flops 21448 | bytes 960 | tf_op jit(solution)/shard_map/reduce_min | solution.py:285
  2.0 16.1 %shard_map.77 = (bf16[128,128]{1,0:T(8,128)(2,1)}, bf16[8,80,128]{2,1,0:T(8,128)(2,1)}) custom-call(s32[56]{0:T(128)} %select_reduce_fusion.inverse_ref, s32[1,128]{1,0:T(1,128)} %assign_ref.1, bf16[128,2048]{1,0:T(8,128)(2,1)} %acts_hbm.1, bf16[128,7168]{1,0:T(8,128)(2,1)} %grads_hbm.1, bf16[64,8192]{1,0:T(8,128)(2,1)} %bitcast.3, bf16[128,64,128]{2,1,0:T(8,128)(2,1)} %bitcast.2), custom_call_target="tpu_custom_call" | custom-call | tf_op jit(solution)/shard_map/pallas_call | solution.py:286
  18.1 0.0 copy-start
  18.1 0.9 %copy-done = bf16[8,80,128]{2,1,0:T(8,128)(2,1)S(1)} copy-done((bf16[8,80,128]{2,1,0:T(8,128)(2,1)S(1)}, bf16[8,80,128]{2,1,0:T(8,128)(2,1)}, u32[]{:S(2)}) %copy-start) | copy-done | bytes 163864
  19.0 0.0 copy-start.1
  19.0 0.8 %copy-done.1 = bf16[128,128]{1,0:T(8,128)(2,1)S(1)} copy-done((bf16[128,128]{1,0:T(8,128)(2,1)S(1)}, bf16[128,128]{1,0:T(8,128)(2,1)}, u32[]{:S(2)}) %copy-start.1) | copy-done | bytes 32792
  19.7 23.4 %shard_map.78 = (bf16[32,4096]{1,0:T(8,128)(2,1)}, f32[2,512,512]{2,1,0:T(8,128)}) custom-call(bf16[8,80,128]{2,1,0:T(8,128)(2,1)S(1)} %copy-done, bf16[128,128]{1,0:T(8,128)(2,1)S(1)} %copy-done.1), custom_call_target="tpu_custom_call" | custom-call | tf_op jit(solution)/shard_map/pallas_call | solution.py:310
  (1 shorter events, 0.0 us)
Async XLA Ops:
  18.1 0.9 %copy-start = (bf16[8,80,128]{2,1,0:T(8,128)(2,1)S(1)}, bf16[8,80,128]{2,1,0:T(8,128)(2,1)}, u32[]{:S(2)}) copy-start(bf16[8,80,128]{2,1,0:T(8,128)(2,1)} %get-tuple-element.4.gath_hbm) | copy-start | bytes 491524
  19.0 0.8 %copy-start.1 = (bf16[128,128]{1,0:T(8,128)(2,1)S(1)}, bf16[128,128]{1,0:T(8,128)(2,1)}, u32[]{:S(2)}) copy-start(bf16[128,128]{1,0:T(8,128)(2,1)} %get-tuple-element.5.full_hbm) | copy-start | bytes 98308

commit v3 on v2

--- a/solution.py
+++ b/solution.py
@@ -113,40 +113,55 @@
     scale = [jnp.zeros((half, TILE), F32) for _ in range(2)]
     tops = [row[:half] for row in rows]
     ends = [row[half:] for row in rows]
-    for k in range(STEP):
+
+    def spread(x, at):
+        return jnp.broadcast_to(x[at:at + 1, :], (half, TILE))
+
+    def reduce_rows(low, at, top, end):
+        if low:
+            top = jnp.where(sub > at, top, 0.0)
+        else:
+            end = jnp.where(sub > at, end, 0.0)
+        for t in range(len(rows)):
+            row = spread(tops[t] if low else ends[t], at)
+            if low and at < half - 1:
+                tops[t] = tops[t] - top * row
+            ends[t] = ends[t] - end * row
+
+    for k in range(0, STEP, 2):
         low, at = k < half, k % half
-        pivot = heads[k] if low else tails[k]
-        root = jnp.broadcast_to(lax.rsqrt(pivot[at:at + 1, :]), (half, TILE))
-        inv = root * root
-        scale[k // half] = jnp.where(sub == at, root, scale[k // half])
-        if k == STEP - 1:
-            break
-        end = tails[k] * inv
+        x, y = (heads[k], heads[k + 1]) if low else (tails[k], tails[k + 1])
+        p, e, q = spread(x, at), spread(x, at + 1), spread(y, at + 1)
+        det = p * q - e * e
+        root_p, root_d = lax.rsqrt(p), lax.rsqrt(det)
+        inv_p = root_p * root_p
+        inv_s = (root_d * root_d) * p
+        ratio = e * inv_p
+        scale[k // half] = jnp.where(sub == at, root_p, scale[k // half])
+        scale[k // half] = jnp.where(sub == at + 1, root_d * (p * root_p), scale[k // half])
+        end_x = tails[k] * inv_p
+        tails[k + 1] = tails[k + 1] - tails[k] * ratio
+        end_y = tails[k + 1] * inv_s
+        top_x = top_y = None
         if low:
-            top = heads[k] * inv
-            for j in range(k + 1, half):
-                entry = heads[k][j:j + 1, :]
-                heads[j] = heads[j] - top * entry
-                tails[j] = tails[j] - end * entry
-            for j in range(half, STEP):
-                tails[j] = tails[j] - end * tails[k][j - half:j - half + 1, :]
-            top = jnp.where(sub > at, top, 0.0)
-            for t in range(len(rows)):
-                row = tops[t][at:at + 1, :]
-                if at < half - 1:
-                    tops[t] = tops[t] - top * row
-                ends[t] = ends[t] - end * row
-        else:
-            for j in range(k + 1, STEP):
-                tails[j] = tails[j] - end * tails[k][j - half:j - half + 1, :]
-            end = jnp.where(sub > at, end, 0.0)
-            for t in range(len(rows)):
-                ends[t] = ends[t] - end * ends[t][at:at + 1, :]
+            top_x = heads[k] * inv_p
+            heads[k + 1] = heads[k + 1] - heads[k] * ratio
+            top_y = heads[k + 1] * inv_s
+        for j in range(k + 2, STEP):
+            if j < half:
+                xj, yj = spread(heads[k], j), spread(heads[k + 1], j)
+                heads[j] = (heads[j] - top_x * xj) - top_y * yj
+            else:
+                xj, yj = spread(tails[k], j - half), spread(tails[k + 1], j - half)
+            tails[j] = (tails[j] - end_x * xj) - end_y * yj
+        reduce_rows(low, at, top_x, end_x)
+        if k + 1 < STEP - 1:
+            reduce_rows(low, at + 1, top_y, end_y)
     return [jnp.concatenate([top * scale[0], end * scale[1]], axis=0) for top, end in zip(tops, ends)]
 
 
 def factor_kernel(mp, k_in, k_out, need, gath_hbm, full_hbm, feat_hbm, factor_hbm,
-                  gath_ref, full_ref, feat_ref, factor_ref, ft, inf, cov, panel, upper, ins, fsem, osem):
+                  gath_ref, full_ref, feat_ref, factor_ref, ft, inf, cov, panel, upper, left, right, ins, fsem, osem):
     m = lax.axis_index("mp")
     dp, _, ex = gath_ref.shape
     nb = factor_ref.shape[0]
@@ -167,9 +182,9 @@
     lane = lax.broadcasted_iota(jnp.int32, (mine, TILE), 1)
     outs = jnp.concatenate([coords[:, k_in:], coords[:, k_in:]], axis=1)
     for t in range(k_in // 2):
-        left = jnp.broadcast_to(coords[:, 2 * t:2 * t + 1], (mine, TILE))
-        right = jnp.broadcast_to(coords[:, 2 * t + 1:2 * t + 2], (mine, TILE))
-        feat_ref[:, t * TILE:(t + 1) * TILE] = (jnp.where(lane < k_out, left, right) * outs).astype(BF16)
+        even = jnp.broadcast_to(coords[:, 2 * t:2 * t + 1], (mine, TILE))
+        odd = jnp.broadcast_to(coords[:, 2 * t + 1:2 * t + 2], (mine, TILE))
+        feat_ref[:, t * TILE:(t + 1) * TILE] = (jnp.where(lane < k_out, even, odd) * outs).astype(BF16)
 
     feat_store = pltpu.make_async_copy(feat_ref, feat_hbm, fsem)
     feat_store.start()
@@ -234,10 +249,10 @@
                     upper[c, t, lo:hi, :] = rows[t]
                 if hi < TILE:
                     h, l = parts[0]
-                    left = jnp.concatenate([h, h, l, l], axis=0)[:, hi:].astype(BF16)
-                    right = jnp.concatenate(
+                    lhs = jnp.concatenate([h, h, l, l], axis=0)[:, hi:].astype(BF16)
+                    rhs = jnp.concatenate(
                         [jnp.concatenate([h, l, h, l], axis=0) for h, l in parts], axis=1).astype(BF16)
-                    update = dot_tn(left, right)
+                    update = dot_tn(lhs, rhs)
                     for t in range(tiles):
                         panel[c, t, hi:, :] = panel[c, t, hi:, :] - update[:, t * TILE:(t + 1) * TILE]
         tri = (lax.broadcasted_iota(jnp.int32, (TILE, TILE), 1)
@@ -247,17 +262,24 @@
             for t in range(1, tiles):
                 factor_ref[c, at, tile_at(t)] = jnp.where(b + t < tiles, upper[c, t], 0.0)
             pltpu.make_async_copy(factor_ref.at[c, at], factor_hbm.at[c, at], osem.at[c, b]).start()
+        @pl.when(b < tiles - 1)
+        def _():
+            for c in range(nb):
+                for t in range(tiles):
+                    h, l = split(upper[c, t])
+                    h, l = h.astype(BF16), l.astype(BF16)
+                    for n, (a, z) in enumerate(((h, h), (h, l), (l, h), (l, l))):
+                        left[c, n * TILE:(n + 1) * TILE, t * TILE:(t + 1) * TILE] = a
+                        right[c, n * TILE:(n + 1) * TILE, t * TILE:(t + 1) * TILE] = z
+
         for i in range(1, tiles):
             @pl.when(b + i < tiles)
             def _():
                 here = pl.ds(pl.multiple_of(lax.rem(b + i, tiles) * TILE, TILE), TILE)
                 for c in range(nb):
-                    h, l = split(upper[c, i])
-                    left = jnp.concatenate([h, h, l, l], axis=0).astype(BF16)
+                    update = dot_tn(left[c, :, i * TILE:(i + 1) * TILE], right[c, :, i * TILE:])
                     for t in range(i, tiles):
-                        h, l = split(upper[c, t])
-                        right = jnp.concatenate([h, l, h, l], axis=0).astype(BF16)
-                        cov[c, here, tile_at(t)] = cov[c, here, tile_at(t)] - dot_tn(left, right)
+                        cov[c, here, tile_at(t)] = cov[c, here, tile_at(t)] - update[:, (t - i) * TILE:(t - i + 1) * TILE]
         return carry
 
     lax.fori_loop(0, tiles, block_row, 0)
@@ -323,11 +345,13 @@
             pltpu.VMEM((nb, FB, FB), F32),
             pltpu.VMEM((nb, FB // TILE, TILE, TILE), F32),
             pltpu.VMEM((nb, FB // TILE, TILE, TILE), F32),
+            pltpu.VMEM((nb, 4 * TILE, FB), BF16),
+            pltpu.VMEM((nb, 4 * TILE, FB), BF16),
             pltpu.SemaphoreType.DMA((2,)),
             pltpu.SemaphoreType.DMA(()),
             pltpu.SemaphoreType.DMA((nb, FB // TILE)),
         ],
-        compiler_params=pltpu.CompilerParams(vmem_limit_bytes=48 << 20),
+        compiler_params=pltpu.CompilerParams(vmem_limit_bytes=63 << 20),
     )(gath, full)
     return features, factor
 

time: 43.4 us -> 43.1 us (level)
  local copies, waits for them, and re-layouts: 1.67 us -> 0 us
  Pallas kernels: 39.5 us -> 40.9 us
    unnamed x4 -> x0, local copies, waits for them, and re-layouts: 1.67 us -> none
    pallas_call x1, Pallas kernels: 23.4 us -> 24.9 us  [shards(): pl.pallas_call(functools.partial(factor_kernel, mp, k_in, k_out, need), o...]
where the time goes in v3:
time: 43.1 us; the launch traced here: 42.9 us
  Pallas kernels  40.9 us (95%)
  other arithmetic  1.36 us (3%)
  between operations  0.65 us (2%)
    pallas_call x1, Pallas kernels, shards(): pl.pallas_call(functools.partial(factor_kernel, mp, k_in, k_out, need), o...  24.9 us
    pallas_call x1, Pallas kernels, shards(): pl.pallas_call(functools.partial(coords_kernel, mp, dp, need), out_shape=...  16.1 us
    reduce_min x1, other arithmetic, shards(): jnp.min(jnp.where(block_index[None, :] == ids[:, None], order[None, :], n...  1.36 us

profile of v3, /device:TPU:0, one launch (start us, length us, event | category | flops | bytes accessed | tf_op | source)
XLA Modules:
  0.0 42.9 jit_solution(7763449371750597860)
XLA Ops:
  0.6 1.4 %select_reduce_fusion.inverse_ref = s32[56]{0:T(128)} fusion(s32[128]{0:T(128)} %param.10, s32[56]{0:T(128)S(1)} %iota_add_fusion), kind=kLoop, calls=%fused_computation | loop fusion | flops 21448 | bytes 960 | tf_op jit(solution)/shard_map/reduce_min | solution.py:307
  2.0 16.1 %shard_map.77 = (bf16[128,128]{1,0:T(8,128)(2,1)}, bf16[8,80,128]{2,1,0:T(8,128)(2,1)}) custom-call(s32[56]{0:T(128)} %select_reduce_fusion.inverse_ref, s32[1,128]{1,0:T(1,128)} %assign_ref.1, bf16[128,2048]{1,0:T(8,128)(2,1)} %acts_hbm.1, bf16[128,7168]{1,0:T(8,128)(2,1)} %grads_hbm.1, bf16[64,8192]{1,0:T(8,128)(2,1)} %bitcast.3, bf16[128,64,128]{2,1,0:T(8,128)(2,1)} %bitcast.2), custom_call_target="tpu_custom_call" | custom-call | tf_op jit(solution)/shard_map/pallas_call | solution.py:308
  18.1 24.9 %shard_map.78 = (bf16[32,4096]{1,0:T(8,128)(2,1)}, f32[2,512,512]{2,1,0:T(8,128)}) custom-call(bf16[8,80,128]{2,1,0:T(8,128)(2,1)} %get-tuple-element.4.gath_hbm, bf16[128,128]{1,0:T(8,128)(2,1)} %get-tuple-element.5.full_hbm), custom_call_target="tpu_custom_call" | custom-call | tf_op jit(solution)/shard_map/pallas_call | solution.py:332
  (1 shorter events, 0.0 us)

commit v4 on v3

--- a/solution.py
+++ b/solution.py
@@ -100,11 +100,6 @@
     gath_ref[d] = slab[...]
     for copy in copies:
         copy.wait()
-
-
-def split(x):
-    high = x.astype(BF16).astype(F32)
-    return high, x - high
 
 
 def eliminate(heads, tails, rows):
@@ -161,7 +156,7 @@
 
 
 def factor_kernel(mp, k_in, k_out, need, gath_hbm, full_hbm, feat_hbm, factor_hbm,
-                  gath_ref, full_ref, feat_ref, factor_ref, ft, inf, cov, panel, upper, left, right, ins, fsem, osem):
+                  gath_ref, full_ref, feat_ref, factor_ref, ft, inf, cov, left, right, ins, fsem, osem):
     m = lax.axis_index("mp")
     dp, _, ex = gath_ref.shape
     nb = factor_ref.shape[0]
@@ -206,88 +201,75 @@
 
     total = dp * ex
     chunk = min(total, 1024)
-    half = FB // 2
-    diag = jnp.where(lax.broadcasted_iota(jnp.int32, (half, half), 0)
-                     == lax.broadcasted_iota(jnp.int32, (half, half), 1), DAMPING, 0.0)
+    mid = FB // 2
+    diag = jnp.where(lax.broadcasted_iota(jnp.int32, (mid, mid), 0)
+                     == lax.broadcasted_iota(jnp.int32, (mid, mid), 1), DAMPING, 0.0)
     for c in range(nb):
         for i in range(2):
             for j in range(i, 2):
                 def piece(n):
                     at = pl.ds(pl.multiple_of(n * chunk, chunk), chunk)
-                    return dot_nt(ft[c * FB + i * half:c * FB + (i + 1) * half, at],
-                                  ft[c * FB + j * half:c * FB + (j + 1) * half, at])
+                    return dot_nt(ft[c * FB + i * mid:c * FB + (i + 1) * mid, at],
+                                  ft[c * FB + j * mid:c * FB + (j + 1) * mid, at])
                 gram = piece(0)
                 if total > chunk:
                     gram = lax.fori_loop(1, total // chunk, lambda n, acc: acc + piece(n), gram)
                 gram = gram * (1.0 / total)
                 if i == j:
                     gram = gram + diag
-                cov[c, i * half:(i + 1) * half, j * half:(j + 1) * half] = gram
-
-    def block_row(b, carry):
-        at = pl.ds(pl.multiple_of(b * TILE, TILE), TILE)
-
-        def tile_at(t):
-            return pl.ds(pl.multiple_of(lax.rem(b + t, tiles) * TILE, TILE), TILE)
-
+                cov[c, i * mid:(i + 1) * mid, j * mid:(j + 1) * mid] = gram
+
+    tri = (lax.broadcasted_iota(jnp.int32, (TILE, TILE), 1)
+           >= lax.broadcasted_iota(jnp.int32, (TILE, TILE), 0))
+    half = STEP // 2
+    stores = []
+    for b in range(tiles):
+        lead, count = b * TILE, tiles - b
         for c in range(nb):
-            for t in range(tiles):
-                panel[c, t] = cov[c, at, tile_at(t)]
+            if b:
+                factor_ref[c, lead:lead + TILE, :lead] = jnp.zeros((TILE, lead), F32)
         for s in range(TILE // STEP):
-            lo, hi = s * STEP, (s + 1) * STEP
+            lo, hi = lead + s * STEP, lead + (s + 1) * STEP
+            at = s * STEP
             cols = []
             for c in range(nb):
-                pivot = panel[c, 0, lo:hi, :]
-                half = STEP // 2
+                pivot = cov[c, lo:hi, lead:lead + TILE]
                 cols.append((
-                    [jnp.broadcast_to(pivot[:half, lo + j:lo + j + 1], (half, TILE)) for j in range(half)],
-                    [jnp.broadcast_to(pivot[half:, lo + j:lo + j + 1], (half, TILE)) for j in range(STEP)]))
+                    [jnp.broadcast_to(pivot[:half, at + j:at + j + 1], (half, TILE)) for j in range(half)],
+                    [jnp.broadcast_to(pivot[half:, at + j:at + j + 1], (half, TILE)) for j in range(STEP)]))
             for c in range(nb):
-                rows = eliminate(*cols[c], [panel[c, t, lo:hi, :] for t in range(tiles)])
-                parts = [split(row) for row in rows]
-                for t in range(tiles):
-                    upper[c, t, lo:hi, :] = rows[t]
-                if hi < TILE:
-                    h, l = parts[0]
-                    lhs = jnp.concatenate([h, h, l, l], axis=0)[:, hi:].astype(BF16)
+                rows = eliminate(*cols[c], [cov[c, lo:hi, lead + t * TILE:lead + (t + 1) * TILE] for t in range(count)])
+                high = [row.astype(BF16) for row in rows]
+                low = [(row - h.astype(F32)).astype(BF16) for row, h in zip(rows, high)]
+                for t in range(count):
+                    row = rows[t]
+                    if t == 0:
+                        row = jnp.where(tri[at:at + STEP], row, 0.0)
+                    factor_ref[c, lo:hi, lead + t * TILE:lead + (t + 1) * TILE] = row
+                if hi < lead + TILE:
+                    lhs = jnp.concatenate([high[0], high[0], low[0], low[0]], axis=0)[:, at + STEP:]
                     rhs = jnp.concatenate(
-                        [jnp.concatenate([h, l, h, l], axis=0) for h, l in parts], axis=1).astype(BF16)
-                    update = dot_tn(lhs, rhs)
-                    for t in range(tiles):
-                        panel[c, t, hi:, :] = panel[c, t, hi:, :] - update[:, t * TILE:(t + 1) * TILE]
-        tri = (lax.broadcasted_iota(jnp.int32, (TILE, TILE), 1)
-               >= lax.broadcasted_iota(jnp.int32, (TILE, TILE), 0))
+                        [jnp.concatenate([h, l, h, l], axis=0) for h, l in zip(high, low)], axis=1)
+                    cov[c, hi:lead + TILE, lead:] = cov[c, hi:lead + TILE, lead:] - dot_tn(lhs, rhs)
+                if count > 1:
+                    for t in range(1, count):
+                        for n in range(4):
+                            to = slice(n * TILE + at, n * TILE + at + STEP)
+                            left[c, to, t * TILE:(t + 1) * TILE] = (high if n < 2 else low)[t]
+                            right[c, to, t * TILE:(t + 1) * TILE] = (low if n % 2 else high)[t]
         for c in range(nb):
-            factor_ref[c, at, tile_at(0)] = jnp.where(tri, upper[c, 0], 0.0)
-            for t in range(1, tiles):
-                factor_ref[c, at, tile_at(t)] = jnp.where(b + t < tiles, upper[c, t], 0.0)
-            pltpu.make_async_copy(factor_ref.at[c, at], factor_hbm.at[c, at], osem.at[c, b]).start()
-        @pl.when(b < tiles - 1)
-        def _():
+            store = pltpu.make_async_copy(
+                factor_ref.at[c, pl.ds(lead, TILE)], factor_hbm.at[c, pl.ds(lead, TILE)], osem.at[c, b])
+            store.start()
+            stores.append(store)
+        for i in range(1, count):
+            here = lead + i * TILE
             for c in range(nb):
-                for t in range(tiles):
-                    h, l = split(upper[c, t])
-                    h, l = h.astype(BF16), l.astype(BF16)
-                    for n, (a, z) in enumerate(((h, h), (h, l), (l, h), (l, l))):
-                        left[c, n * TILE:(n + 1) * TILE, t * TILE:(t + 1) * TILE] = a
-                        right[c, n * TILE:(n + 1) * TILE, t * TILE:(t + 1) * TILE] = z
-
-        for i in range(1, tiles):
-            @pl.when(b + i < tiles)
-            def _():
-                here = pl.ds(pl.multiple_of(lax.rem(b + i, tiles) * TILE, TILE), TILE)
-                for c in range(nb):
-                    update = dot_tn(left[c, :, i * TILE:(i + 1) * TILE], right[c, :, i * TILE:])
-                    for t in range(i, tiles):
-                        cov[c, here, tile_at(t)] = cov[c, here, tile_at(t)] - update[:, (t - i) * TILE:(t - i + 1) * TILE]
-        return carry
-
-    lax.fori_loop(0, tiles, block_row, 0)
+                update = dot_tn(left[c, :, i * TILE:(i + 1) * TILE], right[c, :, i * TILE:count * TILE])
+                cov[c, here:here + TILE, here:] = cov[c, here:here + TILE, here:] - update
+    for store in stores:
+        store.wait()
     feat_store.wait()
-    for c in range(nb):
-        for b in range(tiles):
-            at = pl.ds(b * TILE, TILE)
-            pltpu.make_async_copy(factor_ref.at[c, at], factor_hbm.at[c, at], osem.at[c, b]).wait()
 
 
 def shards(acts, grads, proj_in, block_vals, block_index, assign):
@@ -343,8 +325,6 @@
             pltpu.VMEM((nb * FB, dp * ex), BF16),
             pltpu.VMEM((need, ex), F32),
             pltpu.VMEM((nb, FB, FB), F32),
-            pltpu.VMEM((nb, FB // TILE, TILE, TILE), F32),
-            pltpu.VMEM((nb, FB // TILE, TILE, TILE), F32),
             pltpu.VMEM((nb, 4 * TILE, FB), BF16),
             pltpu.VMEM((nb, 4 * TILE, FB), BF16),
             pltpu.SemaphoreType.DMA((2,)),

time: 43.1 us -> 39.9 us (0.926)
  Pallas kernels: 40.9 us -> 37.8 us
    pallas_call x1, Pallas kernels: 24.9 us -> 21.7 us  [shards(): pl.pallas_call(functools.partial(factor_kernel, mp, k_in, k_out, need), o...]
where the time goes in v4:
time: 39.9 us; the launch traced here: 39.8 us
  Pallas kernels  37.8 us (95%)
  other arithmetic  1.36 us (3%)
  between operations  0.65 us (2%)
    pallas_call x1, Pallas kernels, shards(): pl.pallas_call(functools.partial(factor_kernel, mp, k_in, k_out, need), o...  21.7 us
    pallas_call x1, Pallas kernels, shards(): pl.pallas_call(functools.partial(coords_kernel, mp, dp, need), out_shape=...  16.1 us
    reduce_min x1, other arithmetic, shards(): jnp.min(jnp.where(block_index[None, :] == ids[:, None], order[None, :], n...  1.36 us

profile of v4, /device:TPU:0, one launch (start us, length us, event | category | flops | bytes accessed | tf_op | source)
XLA Modules:
  0.0 39.8 jit_solution(16162408740164467174)
XLA Ops:
  0.6 1.4 %select_reduce_fusion.inverse_ref = s32[56]{0:T(128)} fusion(s32[128]{0:T(128)} %param.10, s32[56]{0:T(128)S(1)} %iota_add_fusion), kind=kLoop, calls=%fused_computation | loop fusion | flops 21448 | bytes 960 | tf_op jit(solution)/shard_map/reduce_min | solution.py:289
  2.0 16.1 %shard_map.77 = (bf16[128,128]{1,0:T(8,128)(2,1)}, bf16[8,80,128]{2,1,0:T(8,128)(2,1)}) custom-call(s32[56]{0:T(128)} %select_reduce_fusion.inverse_ref, s32[1,128]{1,0:T(1,128)} %assign_ref.1, bf16[128,2048]{1,0:T(8,128)(2,1)} %acts_hbm.1, bf16[128,7168]{1,0:T(8,128)(2,1)} %grads_hbm.1, bf16[64,8192]{1,0:T(8,128)(2,1)} %bitcast.3, bf16[128,64,128]{2,1,0:T(8,128)(2,1)} %bitcast.2), custom_call_target="tpu_custom_call" | custom-call | tf_op jit(solution)/shard_map/pallas_call | solution.py:290
  18.1 21.7 %shard_map.78 = (bf16[32,4096]{1,0:T(8,128)(2,1)}, f32[2,512,512]{2,1,0:T(8,128)}) custom-call(bf16[8,80,128]{2,1,0:T(8,128)(2,1)} %get-tuple-element.4.gath_hbm, bf16[128,128]{1,0:T(8,128)(2,1)} %get-tuple-element.5.full_hbm), custom_call_target="tpu_custom_call" | custom-call | tf_op jit(solution)/shard_map/pallas_call | solution.py:314
  (1 shorter events, 0.0 us)
